TPU v7x, 32 devices: a whole 2x2x4 slice. The times are simulated.
32 devices in a mesh: dp: 8 (over y, x, core), tensor: 4 (over z).
Axes of the slice: x: 2, y: 2, z: 4, core: 2. Of those that a mesh axis runs over, the one named last changes fastest.
Arguments:
- hidden_state_input: bfloat16 [4096, 3584], P(('dp', 'tensor')), may hold values from -500 to 500
- token_embedding_input: bfloat16 [4096, 3584], P(('dp', 'tensor')), may hold values from -500 to 500
- input_norm_gain: float32 [7168], replicated, may hold values from 0.1 to 1.9
- query_projection_weight: bfloat16 [7168, 3584], P('dp', 'tensor'), may hold values from -0.0625 to 0.0625
- key_projection_weight: bfloat16 [7168, 3584], P('dp', 'tensor'), may hold values from -0.0625 to 0.0625
- value_projection_weight: bfloat16 [7168, 3584], P('dp', 'tensor'), may hold values from -0.0625 to 0.0625
- adapter_down_maps: bfloat16 [7168, 384], replicated, may hold values from -1 to 1
- adapter_up_maps: bfloat16 [3, 128, 3584], P(None, None, 'tensor'), may hold values from -2 to 2
- output_projection_weight: bfloat16 [3584, 3584], P('tensor'), may hold values from -0.09375 to 0.09375
- segment: int32 [4096], P('dp'), may hold values from 0 to 3, as said below
- live_token_length: int32 [8], P('dp'), may hold values from 256 to 512, as said below
- request_cache_row: int32 [32], P('dp'), may hold values from 0 to 31, as said below
Outputs:
- block_out: bfloat16 [4096, 3584], P(('dp', 'tensor'))
- kv_cache: bfloat16 [32, 128, 2, 3584], P(None, 'dp', None, 'tensor')
Inputs may be any that keep to these rules, and one draw needn't show every extreme that they name: `segment`: within a stream, the live slots carry request numbers that never fall, every request 0 to 3 appears, each on (129) // 2 to 128 slots, some request in every draw on exactly 128; slots at or past live_token_length hold 3. `live_token_length`: each stream's live tokens; some stream is full in every draw. `request_cache_row`: A permutation of the 32 cache rows.
All inputs are finite; a program needn't handle non-finite values.
Results may differ from a plain program's by a relative error of at most 0.015.
The roundings to bfloat16 on the way count: a program that leaves them out, or rounds other values in their place, can miss the bound.
Values may be sent and summed in bfloat16 or wider, within the bound.
A program may use at most 128 MiB of HBM per device.

v0:
```python
import math

import jax
import jax.numpy as jnp
from jax import lax
from jax.sharding import PartitionSpec as P

HD = 224


epsilon = 1e-05
negative = -1e30


def normalize(hidden_state_input, token_embedding_input, input_norm_gain):
    combined = jnp.concatenate([hidden_state_input, token_embedding_input], 1).astype(jnp.float32)
    factor = lax.rsqrt(jnp.mean(combined * combined, axis=1, keepdims=True) + epsilon)
    return (combined * factor * input_norm_gain).astype(jnp.bfloat16)


def attend_block(query, keys, values, segment, position, live, first, count, key_end):
    heads = query.shape[1] // HD
    block_query = query[first : first + count].reshape(count, heads, HD)
    block_keys = keys.reshape(key_end, heads, HD)
    block_values = values.reshape(key_end, heads, HD)
    scores = jnp.einsum(
        "qhd,khd->hqk", block_query, block_keys, preferred_element_type=jnp.float32
    ) / math.sqrt(HD)
    query_at = position[first : first + count]
    allowed = (
        (segment[first : first + count, None] == segment[None, :key_end])
        & (position[None, :] <= query_at[:, None])
        & (position[None, :] < live)
    )
    scores = jnp.where(allowed[None], scores, negative)
    top = jnp.max(scores, axis=-1, keepdims=True)
    expo = jnp.exp(scores - top)
    weights = (expo / jnp.sum(expo, axis=-1, keepdims=True)).astype(jnp.bfloat16)
    mixed = jnp.einsum("hqk,khd->qhd", weights, block_values, preferred_element_type=jnp.float32)
    mixed = jnp.where((query_at < live)[:, None, None], mixed, 0.0)
    return mixed.astype(jnp.bfloat16).reshape(count, heads * HD)


def body(
    hidden_state_input,
    token_embedding_input,
    input_norm_gain,
    query_projection_weight,
    key_projection_weight,
    value_projection_weight,
    adapter_down_maps,
    adapter_up_maps,
    output_projection_weight,
    segment,
    live_token_length,
    request_cache_row,
):
    adapter_rank_width = adapter_up_maps.shape[1]
    head_cols = query_projection_weight.shape[1]
    normalized_hidden = normalize(hidden_state_input, token_embedding_input, input_norm_gain)
    adapter_update = jnp.dot(
        normalized_hidden, adapter_down_maps, preferred_element_type=jnp.float32
    ).astype(jnp.bfloat16)
    stream_in, stream_low = (
        lax.all_gather(normalized_hidden, "tensor", axis=0, tiled=True),
        lax.all_gather(adapter_update, "tensor", axis=0, tiled=True),
    )
    pieces = (
        lax.all_gather(query_projection_weight, "dp", axis=0, tiled=True),
        lax.all_gather(key_projection_weight, "dp", axis=0, tiled=True),
        lax.all_gather(value_projection_weight, "dp", axis=0, tiled=True),
    )
    folded = tuple(
        (jnp.dot(stream_in, piece, preferred_element_type=jnp.float32) for piece in pieces)
    )
    projected = []
    for adapter_selector in range(3):
        adapter = jnp.dot(
            stream_low[
                :,
                adapter_selector * adapter_rank_width : (adapter_selector + 1) * adapter_rank_width,
            ],
            adapter_up_maps[adapter_selector],
            preferred_element_type=jnp.float32,
        )
        projected.append((folded[adapter_selector] + adapter).astype(jnp.bfloat16))
    query, keys, values = projected
    stream = query.shape[0]
    position = jnp.arange(stream, dtype=jnp.int32)
    live = live_token_length[0]
    block = min(512, stream)
    attended_parts = []
    for block_index in range(stream // block):
        first = block_index * block
        attended_parts.append(
            attend_block(query, keys, values, segment, position, live, first, block, stream)
        )
    attended = jnp.concatenate(attended_parts, 0)
    block_out = lax.psum_scatter(
        jnp.dot(attended, output_projection_weight, preferred_element_type=jnp.float32).astype(
            jnp.bfloat16
        ),
        "tensor",
        scatter_dimension=0,
        tiled=True,
    )
    requests = request_cache_row.shape[0]
    longest = stream // requests
    groups = lax.axis_size("dp")
    piece_len = longest // groups
    numbers = jnp.arange(requests, dtype=jnp.int32)
    membership = ((segment[:, None] == numbers[None, :]) & (position < live)[:, None]).astype(
        jnp.int32
    )
    lengths = jnp.sum(membership, axis=0)
    starts = jnp.cumsum(lengths) - lengths
    offsets = (
        jnp.arange(groups, dtype=jnp.int32)[:, None] * piece_len
        + jnp.arange(piece_len, dtype=jnp.int32)[None, :]
    )
    source_rows = jnp.minimum(starts[None, :, None] + offsets[:, None, :], stream - 1)
    alive_mask = offsets[:, None, :] < lengths[None, :, None]
    stacked = jnp.stack([keys, values], 1).reshape(stream, 2 * head_cols)
    taken = jnp.take(stacked, source_rows.reshape(-1), axis=0)
    taken = jnp.where(alive_mask.reshape(-1)[:, None], taken, jnp.zeros((), jnp.bfloat16))
    taken = taken.reshape(groups, requests, piece_len * 2 * head_cols)
    row_send = jnp.broadcast_to(request_cache_row[None, :], (groups, requests))
    received, received_rows = (
        lax.all_to_all(taken, "dp", split_axis=0, concat_axis=0, tiled=True),
        lax.all_to_all(row_send, "dp", split_axis=0, concat_axis=0, tiled=True),
    )
    total_reqs = groups * requests
    placing = (
        received_rows.reshape(-1)[:, None] == jnp.arange(total_reqs, dtype=jnp.int32)[None, :]
    ).astype(jnp.bfloat16)
    flat_received = received.reshape(total_reqs, piece_len * 2 * head_cols)
    cache_rows = lax.dot_general(
        placing, flat_received, (((0,), (0,)), ((), ())), preferred_element_type=jnp.float32
    )
    kv_cache = cache_rows.astype(jnp.bfloat16).reshape(total_reqs, piece_len, 2, head_cols)
    return (block_out, kv_cache)


def solution(mesh):
    return jax.shard_map(
        body,
        mesh=mesh,
        in_specs=(
            P(("dp", "tensor"), None),
            P(("dp", "tensor"), None),
            P(),
            P("dp", "tensor"),
            P("dp", "tensor"),
            P("dp", "tensor"),
            P(),
            P(None, None, "tensor"),
            P("tensor", None),
            P("dp"),
            P("dp"),
            P("dp"),
        ),
        out_specs=(P(("dp", "tensor"), None), P(None, "dp", None, "tensor")),
        check_vma=False,
    )
```

profile of v0, /device:TPU:0, one launch (start us, length us, event | category | flops | bytes accessed | tf_op | source)
XLA Modules:
  0.0 484.6 jit_solution(14439352498564582158)
XLA Ops:
  7.2 1.9 fusion.1
  9.1 3.2 fusion.3
  12.4 0.7 all-gather.7.cloned.1.call-update
  13.2 0.7 all-gather.9.cloned.1.call-update
  13.9 0.5 all-gather.11.cloned.1.call-update
  14.5 0.6 broadcast_in_dim.81
  15.0 5.2 %all-to-all-start = ((s32[8,1,4]{2,1,0:T(1,128)}), s32[8,1,4]{2,1,0:T(1,128)S(1)}, u32[]{:S(2)}, u32[]{:S(2)}) async-start(s32[8,1,4]{2,1,0:T(1,128)} %broadcast_in_dim.81), calls=%async_computation.1 | async-start | bytes 8192 | tf_op jit(solution)/shard_map/all_to_all | solution.py:130
  20.9 0.1 convert_reduce_fusion
  21.0 0.2 reduce-window.8
  21.3 0.1 compare_and_fusion
  21.4 0.3 broadcast_in_dim.82
  21.7 2.2 broadcast_in_dim.83
  23.9 0.3 broadcast_in_dim.84
  24.2 2.2 broadcast_in_dim.85
  26.5 0.1 min.22
  26.6 4.0 convolution_convert_fusion.2
  30.6 20.7 %all_gather.17 = bf16[512,384]{1,0:T(8,128)(2,1)S(1)} all-gather(bf16[128,384]{1,0:T(8,128)(2,1)S(1)} %convolution_convert_fusion.2), channel_id=1, replica_groups=mesh['dp'=8,'tensor'=4] {'tensor'}, dimensions={0}, use_global_device_ids=true | all-gather | bytes 491520 | tf_op jit(solution)/shard_map/all_gather | solution.py:66
  51.4 0.2 fusion.10
  51.6 1.6 fusion.15
  53.2 0.4 fusion.13
  53.6 1.6 fusion.11
  55.2 98.8 %all-gather.5.cloned.1.call-done = bf16[512,7168]{1,0:T(8,128)(2,1)} async-done(((bf16[128,7168]{1,0:T(8,128)(2,1)}), bf16[512,7168]{1,0:T(8,128)(2,1)}) %all-gather.5.cloned.1.call-update) | async-done | bytes 7340048 | tf_op jit(solution)/shard_map/all_gather | solution.py:65
  154.0 73.4 %all-gather.7.cloned.1.call-done = bf16[7168,896]{1,0:T(8,128)(2,1)} async-done(((bf16[896,896]{1,0:T(8,128)(2,1)}), bf16[7168,896]{1,0:T(8,128)(2,1)}) %all-gather.7.cloned.1.call-update) | async-done | bytes 12845072 | tf_op jit(solution)/shard_map/all_gather | solution.py:71
  227.4 14.0 %add_convert_fusion.2 = bf16[512,896]{1,0:T(8,128)(2,1)S(1)} fusion(f32[512,896]{1,0:T(8,128)} %fusion.15, bf16[512,7168]{1,0:T(8,128)(2,1)} %all-gather.5.cloned.1.call-done, bf16[7168,896]{1,0:T(8,128)(2,1)} %all-gather.7.cloned.1.call-done), kind=kOutput, calls=%fused_computation.23 | convolution fusion | flops 6577586176 | bytes 22937600 | tf_op jit(solution)/shard_map/dot_general | solution.py:74
  241.4 1.3 copy.30
  242.7 59.8 %all-gather.9.cloned.1.call-done = bf16[7168,896]{1,0:T(8,128)(2,1)} async-done(((bf16[896,896]{1,0:T(8,128)(2,1)}), bf16[7168,896]{1,0:T(8,128)(2,1)}) %all-gather.9.cloned.1.call-update) | async-done | bytes 12845072 | tf_op jit(solution)/shard_map/all_gather | solution.py:69
  302.5 12.9 %add_convert_fusion.1 = bf16[512,896]{1,0:T(8,128)(2,1)} fusion(f32[512,896]{1,0:T(8,128)S(1)} %fusion.13, bf16[512,7168]{1,0:T(8,128)(2,1)} %all-gather.5.cloned.1.call-done, bf16[7168,896]{1,0:T(8,128)(2,1)} %all-gather.9.cloned.1.call-done), kind=kOutput, calls=%fused_computation.22 | convolution fusion | flops 6577586176 | bytes 22937600 | tf_op jit(solution)/shard_map/dot_general | solution.py:74
  315.5 2.2 copy.31
  317.7 59.8 %all-gather.11.cloned.1.call-done = bf16[7168,896]{1,0:T(8,128)(2,1)} async-done(((bf16[896,896]{1,0:T(8,128)(2,1)}), bf16[7168,896]{1,0:T(8,128)(2,1)}) %all-gather.11.cloned.1.call-update) | async-done | bytes 12845072 | tf_op jit(solution)/shard_map/all_gather | solution.py:70
  377.6 14.0 %add_convert_fusion = bf16[512,896]{1,0:T(8,128)(2,1)S(1)} fusion(f32[512,896]{1,0:T(8,128)} %fusion.11, bf16[512,7168]{1,0:T(8,128)(2,1)} %all-gather.5.cloned.1.call-done, bf16[7168,896]{1,0:T(8,128)(2,1)} %all-gather.11.cloned.1.call-done), kind=kOutput, calls=%fused_computation.21 | convolution fusion | flops 6577586176 | bytes 22937600 | tf_op jit(solution)/shard_map/dot_general | solution.py:74
  391.6 1.3 copy.32
  392.9 5.2 %fusion.29 = (f32[4,512]{1,0:T(4,128)S(1)}, f32[4,512,512]{1,2,0:T(8,128)}) fusion(pred[512,512]{0,1:T(8,128)(4,1)S(1)} %fusion.10, bf16[512,4,224]{0,2,1:T(8,128)(2,1)} %bitcast.48, bf16[512,4,224]{0,2,1:T(8,128)(2,1)} %bitcast.49), kind=kOutput, calls=%fused_computation.59 | convolution fusion | flops 473956864 | bytes 6299648 | tf_op jit(solution)/shard_map/sub | solution.py:37
  398.1 2.8 select_convert_fusion
  401.0 8.5 %convolution_convert_fusion.1 = bf16[512,3584]{1,0:T(8,128)(2,1)} fusion(bf16[512,896]{0,1:T(8,128)(2,1)S(1)} %bitcast.52, bf16[896,3584]{1,0:T(8,128)(2,1)} %param.20), kind=kOutput, calls=%fused_computation.3 | convolution fusion | flops 3290169344 | bytes 11010048 | tf_op jit(solution)/shard_map/dot_general | solution.py:100
  409.5 1.4 pad_maximum_fusion.1
  410.9 2.4 copy.34
  413.3 2.9 copy.35
  416.2 3.1 gather_fusion
  419.3 3.5 gather.7
  422.9 4.7 select_select_fusion
  427.5 3.6 all-to-all-start.1
  431.1 0.6 broadcast.148
  431.7 0.6 reduce.3
  432.4 22.5 %all-to-all-done.1 = bf16[8,4,28672]{2,1,0:T(4,128)(2,1)S(1)} async-done(((bf16[8,4,28672]{2,1,0:T(4,128)(2,1)}), bf16[8,4,28672]{2,1,0:T(4,128)(2,1)S(1)}, u32[]{:S(2)}, u32[]{:S(2)}) %all-to-all-start.1) | async-done | bytes 1835040 | tf_op jit(solution)/shard_map/all_to_all | solution.py:129
  454.9 1.5 reshape.232
  456.3 2.2 convolution_convert_fusion
  458.6 2.4 reshape.233
  460.9 17.1 %reduce-scatter.2.cloned.1.call-done = bf16[128,3584]{1,0:T(8,128)(2,1)} async-done(((bf16[512,3584]{1,0:T(8,128)(2,1)}), bf16[128,3584]{1,0:T(8,128)(2,1)}) %reduce-scatter.2.cloned.1.call-update) | async-done | bytes 917520 | tf_op jit(solution)/shard_map/reduce_scatter | solution.py:99
  (31 shorter events, 0.5 us)
Async XLA Ops:
  7.2 146.8 %all-gather.5.cloned.1.call-start = ((), (), s32[]{:S(2)}) async-start(), calls=%async_computation.3 | async-start | bytes 9175040 | tf_op jit(solution)/shard_map/all_gather | solution.py:65
  12.3 2.1 copy-start.6
  12.3 8.6 %copy-start.5 = (s32[512]{0:T(512)S(1)}, s32[512]{0:T(512)}, u32[]{:S(2)}) copy-start(s32[512]{0:T(512)} %param.21) | copy-start | bytes 6148
  12.4 215.0 %all-gather.7.cloned.1.call-start = ((), (), s32[]{:S(2)}) async-start(), calls=%async_computation.4 | async-start | bytes 14450688 | tf_op jit(solution)/shard_map/all_gather | solution.py:71
  13.1 289.4 %all-gather.9.cloned.1.call-start = ((), (), s32[]{:S(2)}) async-start(), calls=%async_computation.5 | async-start | bytes 14450688 | tf_op jit(solution)/shard_map/all_gather | solution.py:69
  13.9 12.8 %copy-start = (bf16[128,7168]{1,0:T(8,128)(2,1)S(1)}, bf16[128,7168]{1,0:T(8,128)(2,1)}, u32[]{:S(2)}) copy-start(bf16[128,7168]{1,0:T(8,128)(2,1)} %fusion.3) | copy-start | bytes 5505028
  13.9 363.7 %all-gather.11.cloned.1.call-start = ((), (), s32[]{:S(2)}) async-start(), calls=%async_computation.6 | async-start | bytes 14450688 | tf_op jit(solution)/shard_map/all_gather | solution.py:70
  15.0 412.5 %all-to-all-start = ((s32[8,1,4]{2,1,0:T(1,128)}), s32[8,1,4]{2,1,0:T(1,128)S(1)}, u32[]{:S(2)}, u32[]{:S(2)}) async-start(s32[8,1,4]{2,1,0:T(1,128)} %broadcast_in_dim.81), calls=%async_computation.1 | async-start | bytes 8192 | tf_op jit(solution)/shard_map/all_to_all | solution.py:130
  20.2 457.8 %reduce-scatter.2.cloned.1.call-start = ((), (), s32[]{:S(2)}) async-start(), calls=%async_computation.7 | async-start | bytes 4587520 | tf_op jit(solution)/shard_map/reduce_scatter | solution.py:99
  26.6 25.0 %copy-start.4 = (bf16[3,128,896]{2,1,0:T(8,128)(2,1)S(1)}, bf16[3,128,896]{2,1,0:T(8,128)(2,1)}, u32[]{:S(2)}) copy-start(bf16[3,128,896]{2,1,0:T(8,128)(2,1)} %param.19) | copy-start | bytes 2064388
  391.6 6.5 %copy-start.1 = (bf16[512,896]{1,0:T(8,128)(2,1)}, bf16[512,896]{1,0:T(8,128)(2,1)S(1)}, u32[]{:S(2)}) copy-start(bf16[512,896]{1,0:T(8,128)(2,1)S(1)} %add_convert_fusion) | copy-start | bytes 2752516
  392.9 5.2 %copy-start.3 = (bf16[512,896]{0,1:T(8,128)(2,1)S(1)}, bf16[512,896]{0,1:T(8,128)(2,1)}, u32[]{:S(2)}) copy-start(bf16[512,896]{0,1:T(8,128)(2,1)} %copy.30) | copy-start | bytes 2752516
  419.3 3.6 copy-start.2
  427.5 27.4 %all-to-all-start.1 = ((bf16[8,4,28672]{2,1,0:T(4,128)(2,1)}), bf16[8,4,28672]{2,1,0:T(4,128)(2,1)S(1)}, u32[]{:S(2)}, u32[]{:S(2)}) async-start(bf16[8,4,28672]{2,1,0:T(4,128)(2,1)} %select_select_fusion), calls=%async_computation.2 | async-start | bytes 3670016 | tf_op jit(solution)/shard_map/all_to_all | solution.py:129
Sparse Core Ops, SparseCore 0:
  12.5 141.4 all-gather.4
  155.9 71.4 all-gather.6
  229.3 73.2 all-gather.8
  304.3 73.2 all-gather.10
  409.6 68.3 reduce-scatter.1
where the time goes:
time: 485 us
  waiting for transfers between devices  333 us (69%)
  matrix products  67.4 us (14%)
  local copies, waits for them, and re-layouts  27 us (6%)
  blocking collectives  20.7 us (4%)
  between operations  14.6 us (3%)
  other arithmetic  12.6 us (3%)
  starting transfers between devices  8.96 us (2%)
    all_gather x1, waiting for transfers between devices, body(): lax.all_gather(normalized_hidden, 'tensor', axis=0, tiled=True)  98.8 us
    all_gather x1, waiting for transfers between devices, body(): lax.all_gather(value_projection_weight, 'dp', axis=0, tiled=True)  73.4 us
    all_gather x1, waiting for transfers between devices, body(): lax.all_gather(key_projection_weight, 'dp', axis=0, tiled=True)  59.8 us
    all_gather x1, waiting for transfers between devices, body(): lax.all_gather(query_projection_weight, 'dp', axis=0, tiled=True)  59.8 us
    dot_general x3, matrix products, body(): jnp.dot(stream_in, piece, preferred_element_type=jnp.float32)  41 us
    all_to_all x1, waiting for transfers between devices, body(): lax.all_to_all(taken, 'dp', split_axis=0, concat_axis=0, tiled=True)  22.5 us
    all_gather x1, blocking collectives, body(): lax.all_gather(adapter_update, 'tensor', axis=0, tiled=True)  20.7 us
    reduce_scatter x1, waiting for transfers between devices, body(): lax.psum_scatter(jnp.dot(attended, output_projection_weight, preferred_el...  17.1 us
  transfers between devices with their start and end apart: 7, of which 6 were waited for; matrix products, arithmetic and copies ran while one was open for 21% of the time, Pallas kernels for 0%

commit v1 on v0

--- a/solution.py
+++ b/solution.py
@@ -1,11 +1,322 @@
+import functools
 import math
 
 import jax
 import jax.numpy as jnp
 from jax import lax
+from jax.experimental import pallas as pl
+from jax.experimental.pallas import tpu as pltpu
 from jax.sharding import PartitionSpec as P
 
 HD = 224
+
+
+BF = jnp.bfloat16
+F32 = jnp.float32
+MESH = pl.DeviceIdType.MESH
+
+
+def flip(d, r):
+    return sum(b * ((d // b + r // b) % 2) for b in (1, 2, 4))
+
+
+def project_kernel(
+    depth,
+    n_z,
+    din,
+    x_ref,
+    wk_ref,
+    wv_ref,
+    wq_ref,
+    up_ref,
+    kv_ref,
+    q_ref,
+    xs,
+    ws,
+    acc,
+    loc_sem,
+    x_send,
+    x_recv,
+    own_send,
+    own_recv,
+    fwd_send,
+    fwd_recv,
+    sib_send,
+    sib_recv,
+):
+    d = lax.axis_index("dp")
+    z = lax.axis_index("tensor")
+    near = (flip(d, 2), flip(d, 4))
+    sib = flip(d, 1)
+    cols = wk_ref.shape[1]
+    half = depth // 2
+    mats = (wk_ref, wv_ref, wq_ref)
+    has_left, has_right = z > 0, z < n_z - 1
+
+    barrier = pltpu.get_barrier_semaphore()
+    for other in near + (sib,):
+        pl.semaphore_signal(barrier, inc=1, device_id=(other, z), device_id_type=MESH)
+
+    @pl.when(has_left)
+    def _():
+        pl.semaphore_signal(barrier, inc=1, device_id=(d, z - 1), device_id_type=MESH)
+
+    @pl.when(has_right)
+    def _():
+        pl.semaphore_signal(barrier, inc=1, device_id=(d, z + 1), device_id_type=MESH)
+
+    at_end = (z == 0) | (z == n_z - 1)
+
+    @pl.when(at_end)
+    def _():
+        pl.semaphore_wait(barrier, 4)
+
+    @pl.when(jnp.logical_not(at_end))
+    def _():
+        pl.semaphore_wait(barrier, 5)
+
+    def remote(src, dst, send, recv, target):
+        return pltpu.make_async_remote_copy(
+            src_ref=src,
+            dst_ref=dst,
+            send_sem=send,
+            recv_sem=recv,
+            device_id=target,
+            device_id_type=MESH,
+        )
+
+    def token_copy(way, step):
+        src_z = z - step if way == 0 else z + step
+        to_z = z + 1 if way == 0 else z - 1
+        src = x_ref if step == 0 else xs.at[jnp.clip(src_z, 0, n_z - 1)]
+        return remote(
+            src,
+            xs.at[jnp.clip(src_z, 0, n_z - 1)],
+            x_send.at[way, step],
+            x_recv.at[way, step],
+            (d, jnp.clip(to_z, 0, n_z - 1)),
+        )
+
+    def token_sends(way, step):
+        if way == 0:
+            return (z - step >= 0) & has_right
+        return (z + step <= n_z - 1) & has_left
+
+    def token_start(step):
+        for way in (0, 1):
+
+            @pl.when(token_sends(way, step))
+            def _():
+                token_copy(way, step).start()
+
+    def token_wait_recv(step):
+        for way in (0, 1):
+            arrives = (z - step - 1 >= 0) if way == 0 else (z + step + 1 <= n_z - 1)
+
+            @pl.when(arrives)
+            def _():
+                src_z = z - step - 1 if way == 0 else z + step + 1
+                slot = xs.at[jnp.clip(src_z, 0, n_z - 1)]
+                remote(
+                    slot, slot, x_send.at[way, step], x_recv.at[way, step], (sib, z)
+                ).wait_recv()
+
+    def token_wait_send(step):
+        for way in (0, 1):
+
+            @pl.when(token_sends(way, step))
+            def _():
+                token_copy(way, step).wait_send()
+
+    def block(r, m):
+        return ws.at[r, :, pl.ds(m * cols, cols)]
+
+    def part(r, m, h):
+        return ws.at[r, pl.ds(h * half, half), pl.ds(m * cols, cols)]
+
+    def own_copy(m, a, h):
+        return remote(
+            mats[m].at[pl.ds(h * half, half), :],
+            part(2 << a, m, h),
+            own_send.at[m, a, h],
+            own_recv.at[m, a, h],
+            (near[a], z),
+        )
+
+    def own_start(m):
+        for first in (0, 1):
+            for a in (0, 1):
+                own_copy(m, a, a if first == 0 else 1 - a).start()
+
+    def fwd_copy(m, a):
+        h = a
+        return remote(
+            part(2 << a, m, h),
+            part(6, m, h),
+            fwd_send.at[m, a],
+            fwd_recv.at[m, a],
+            (near[1 - a], z),
+        )
+
+    def fwd_recv_wait(m, a):
+        remote(
+            part(6, m, a), part(6, m, a), fwd_send.at[m, a], fwd_recv.at[m, a], (sib, z)
+        ).wait_recv()
+
+    def sib_copy(m, j):
+        src = mats[m] if j == 0 else block(2 * j, m)
+        return remote(src, block(2 * j + 1, m), sib_send.at[m, j], sib_recv.at[m, j], (sib, z))
+
+    def local_copy(m):
+        return pltpu.make_async_copy(mats[m], block(0, m), loc_sem.at[m])
+
+    x_local = pltpu.make_async_copy(x_ref, xs.at[z], loc_sem.at[3])
+
+    token_start(0)
+    own_start(0)
+    own_start(1)
+    x_local.start()
+    for m in range(3):
+        local_copy(m).start()
+    for m in range(2):
+        sib_copy(m, 0).start()
+
+    def take_own(m):
+        for a in (0, 1):
+            own_copy(m, a, a).wait_recv()
+            fwd_copy(m, a).start()
+        for a in (0, 1):
+            own_copy(m, a, 1 - a).wait_recv()
+            sib_copy(m, a + 1).start()
+
+    def take_diag(m):
+        for a in (0, 1):
+            fwd_recv_wait(m, a)
+        sib_copy(m, 3).start()
+
+    take_own(0)
+    own_start(2)
+    sib_copy(2, 0).start()
+    token_wait_recv(0)
+    token_start(1)
+    take_own(1)
+    take_diag(0)
+    token_wait_recv(1)
+    token_start(2)
+    token_wait_recv(2)
+    x_local.wait()
+    for m in range(3):
+        local_copy(m).wait()
+    take_own(2)
+    take_diag(1)
+    for m in range(2):
+        for j in range(4):
+            sib_copy(m, j).wait_recv()
+
+    rows = q_ref.shape[0]
+    rank = up_ref.shape[1]
+
+    def tokens(r):
+        at = pl.multiple_of(flip(d, r) * depth, 128)
+        return xs[:, :, pl.ds(at, depth)].reshape(rows, depth)
+
+    adapter = (1, 2, 0)
+
+    def low(m):
+        at = din + adapter[m] * rank
+        return xs[:, :, at : at + rank].reshape(rows, rank)
+
+    for m in range(2):
+        for c in range(cols // 128):
+            lo = m * cols + c * 128
+            acc[:, pl.ds(lo, 128)] = jnp.dot(
+                low(m), up_ref[adapter[m], :, c * 128 : (c + 1) * 128], preferred_element_type=F32
+            )
+
+    wide = 256
+
+    def kv_tile(t, carry):
+        at = pl.multiple_of(t * wide, 128)
+        tile = pl.ds(at, wide)
+
+        def add(r, c):
+            acc[:, tile] += jnp.dot(tokens(r), ws[r, :, tile], preferred_element_type=F32)
+            return c
+
+        lax.fori_loop(0, 8, add, 0)
+        kv_ref[:, tile] = acc[:, tile].astype(BF)
+        return carry
+
+    lax.fori_loop(0, 2 * cols // wide, kv_tile, 0)
+
+    for c in range(cols // 128):
+        acc[:, c * 128 : (c + 1) * 128] = jnp.dot(
+            low(2), up_ref[adapter[2], :, c * 128 : (c + 1) * 128], preferred_element_type=F32
+        )
+    for j in range(3):
+        sib_copy(2, j).wait_recv()
+
+    def q_add(r, c):
+        for lo in range(0, cols, wide):
+            width = min(wide, cols - lo)
+            acc[:, lo : lo + width] += jnp.dot(
+                tokens(r), ws[r, :, 2 * cols + lo : 2 * cols + lo + width], preferred_element_type=F32
+            )
+        return c
+
+    lax.fori_loop(0, 6, q_add, 0)
+    take_diag(2)
+    q_add(6, 0)
+    sib_copy(2, 3).wait_recv()
+    q_add(7, 0)
+    q_ref[...] = acc[:, :cols].astype(BF)
+
+    for step in range(n_z - 1):
+        token_wait_send(step)
+    for m in range(3):
+        for a in (0, 1):
+            for h in (0, 1):
+                own_copy(m, a, h).wait_send()
+            fwd_copy(m, a).wait_send()
+        for j in range(4):
+            sib_copy(m, j).wait_send()
+
+
+def project(x, wq, wk, wv, up, n_z, din):
+    depth, cols = wk.shape
+    rows = n_z * x.shape[0]
+    dma = pltpu.SemaphoreType.DMA
+    hbm = pl.BlockSpec(memory_space=pl.ANY)
+    vmem = pl.BlockSpec(memory_space=pltpu.VMEM)
+    return pl.pallas_call(
+        functools.partial(project_kernel, depth, n_z, din),
+        out_shape=(
+            jax.ShapeDtypeStruct((rows, 2 * cols), BF),
+            jax.ShapeDtypeStruct((rows, cols), BF),
+        ),
+        in_specs=[hbm, hbm, hbm, hbm, vmem],
+        out_specs=(vmem, vmem),
+        scratch_shapes=[
+            pltpu.VMEM((n_z,) + x.shape, BF),
+            pltpu.VMEM((8, depth, 3 * cols), BF),
+            pltpu.VMEM((rows, 2 * cols), F32),
+            dma((4,)),
+            dma((2, 3)),
+            dma((2, 3)),
+            dma((3, 2, 2)),
+            dma((3, 2, 2)),
+            dma((3, 2)),
+            dma((3, 2)),
+            dma((3, 4)),
+            dma((3, 4)),
+        ],
+        compiler_params=pltpu.CompilerParams(
+            collective_id=0, has_side_effects=True, vmem_limit_bytes=60 * 1024 * 1024
+        ),
+        cost_estimate=pl.CostEstimate(
+            flops=6 * rows * din * cols, bytes_accessed=8 * depth * cols * 6, transcendentals=0
+        ),
+    )(x, wk, wv, wq, up)
 
 
 epsilon = 1e-05
@@ -61,30 +372,46 @@
     adapter_update = jnp.dot(
         normalized_hidden, adapter_down_maps, preferred_element_type=jnp.float32
     ).astype(jnp.bfloat16)
-    stream_in, stream_low = (
-        lax.all_gather(normalized_hidden, "tensor", axis=0, tiled=True),
-        lax.all_gather(adapter_update, "tensor", axis=0, tiled=True),
-    )
-    pieces = (
-        lax.all_gather(query_projection_weight, "dp", axis=0, tiled=True),
-        lax.all_gather(key_projection_weight, "dp", axis=0, tiled=True),
-        lax.all_gather(value_projection_weight, "dp", axis=0, tiled=True),
-    )
-    folded = tuple(
-        (jnp.dot(stream_in, piece, preferred_element_type=jnp.float32) for piece in pieces)
-    )
-    projected = []
-    for adapter_selector in range(3):
-        adapter = jnp.dot(
-            stream_low[
-                :,
-                adapter_selector * adapter_rank_width : (adapter_selector + 1) * adapter_rank_width,
-            ],
-            adapter_up_maps[adapter_selector],
-            preferred_element_type=jnp.float32,
-        )
-        projected.append((folded[adapter_selector] + adapter).astype(jnp.bfloat16))
-    query, keys, values = projected
+    dp, n_z = lax.axis_size("dp"), lax.axis_size("tensor")
+    depth = query_projection_weight.shape[0]
+    if dp == 8 and n_z == 4:
+        own = jnp.concatenate([normalized_hidden, adapter_update], 1)
+        stacked, query = project(
+            own,
+            query_projection_weight,
+            key_projection_weight,
+            value_projection_weight,
+            adapter_up_maps,
+            n_z,
+            dp * depth,
+        )
+        keys, values = stacked[:, :head_cols], stacked[:, head_cols:]
+    else:
+        stream_in, stream_low = (
+            lax.all_gather(normalized_hidden, "tensor", axis=0, tiled=True),
+            lax.all_gather(adapter_update, "tensor", axis=0, tiled=True),
+        )
+        pieces = (
+            lax.all_gather(query_projection_weight, "dp", axis=0, tiled=True),
+            lax.all_gather(key_projection_weight, "dp", axis=0, tiled=True),
+            lax.all_gather(value_projection_weight, "dp", axis=0, tiled=True),
+        )
+        folded = tuple(
+            (jnp.dot(stream_in, piece, preferred_element_type=jnp.float32) for piece in pieces)
+        )
+        projected = []
+        for adapter_selector in range(3):
+            adapter = jnp.dot(
+                stream_low[
+                    :,
+                    adapter_selector * adapter_rank_width : (adapter_selector + 1) * adapter_rank_width,
+                ],
+                adapter_up_maps[adapter_selector],
+                preferred_element_type=jnp.float32,
+            )
+            projected.append((folded[adapter_selector] + adapter).astype(jnp.bfloat16))
+        query, keys, values = projected
+        stacked = jnp.concatenate([keys, values], 1)
     stream = query.shape[0]
     position = jnp.arange(stream, dtype=jnp.int32)
     live = live_token_length[0]
@@ -113,14 +440,14 @@
         jnp.int32
     )
     lengths = jnp.sum(membership, axis=0)
-    starts = jnp.cumsum(lengths) - lengths
+    earlier = numbers[:, None] < numbers[None, :]
+    starts = jnp.sum(jnp.where(earlier, lengths[:, None], 0), axis=0)
     offsets = (
         jnp.arange(groups, dtype=jnp.int32)[:, None] * piece_len
         + jnp.arange(piece_len, dtype=jnp.int32)[None, :]
     )
     source_rows = jnp.minimum(starts[None, :, None] + offsets[:, None, :], stream - 1)
     alive_mask = offsets[:, None, :] < lengths[None, :, None]
-    stacked = jnp.stack([keys, values], 1).reshape(stream, 2 * head_cols)
     taken = jnp.take(stacked, source_rows.reshape(-1), axis=0)
     taken = jnp.where(alive_mask.reshape(-1)[:, None], taken, jnp.zeros((), jnp.bfloat16))
     taken = taken.reshape(groups, requests, piece_len * 2 * head_cols)

time: 485 us -> 309 us (0.64)
  waiting for transfers between devices: 333 us -> 40.9 us
  Pallas kernels: 0 us -> 188 us
  matrix products: 67.4 us -> 19.7 us
  blocking collectives: 20.7 us -> 0 us
    all_gather x4 -> x0, waiting for transfers between devices: 292 us -> none  [the longest x1 98.8 us: body(): lax.all_gather(normalized_hidden, 'tensor', axis=0, tiled=True)]
    pallas_call x0 -> x1, Pallas kernels: none -> 188 us  [project(): pl.pallas_call(functools.partial(project_kernel, depth, n_z, din), out_sh...]
    dot_general x6 -> x0, matrix products: 44.6 us -> none  [the longest x3 41 us: body(): jnp.dot(stream_in, piece, preferred_element_type=jnp.float32)]
    all_gather x1 -> x0, blocking collectives: 20.7 us -> none  [body(): lax.all_gather(adapter_update, 'tensor', axis=0, tiled=True)]
  transfers between devices with their start and end apart: 7 -> 3, of which waited for: 6 -> 2; matrix products, arithmetic and copies ran while one was open for 21% -> 18% of each run, Pallas kernels for 0% -> 61%
where the time goes in v1:
time: 309 us; the launch traced here: 308 us
  Pallas kernels  188 us (61%)
  waiting for transfers between devices  40.9 us (13%)
  local copies, waits for them, and re-layouts  24.4 us (8%)
  matrix products  19.7 us (6%)
  between operations  14.8 us (5%)
  other arithmetic  11.5 us (4%)
  starting transfers between devices  8.81 us (3%)
    pallas_call x1, Pallas kernels, project(): pl.pallas_call(functools.partial(project_kernel, depth, n_z, din), out_sh...  188 us
    all_to_all x1, waiting for transfers between devices, body(): lax.all_to_all(taken, 'dp', split_axis=0, concat_axis=0, tiled=True)  22.6 us
    reduce_scatter x1, waiting for transfers between devices, body(): lax.psum_scatter(jnp.dot(attended, output_projection_weight, preferred_el...  18.3 us
    dot_general x1, matrix products, body(): jnp.dot(attended, output_projection_weight, preferred_element_type=jnp.fl...  8.28 us
    gather x2, local copies, waits for them, and re-layouts, body(): taken = jnp.take(stacked, source_rows.reshape(-1), axis=0)  6.67 us
  transfers between devices with their start and end apart: 3, of which 2 were waited for; matrix products, arithmetic and copies ran while one was open for 18% of the time, Pallas kernels for 61%

profile of v1, /device:TPU:0, one launch (start us, length us, event | category | flops | bytes accessed | tf_op | source)
XLA Modules:
  0.0 307.9 jit_solution(12462374132735793734)
XLA Ops:
  7.2 1.3 broadcast_in_dim.96
  8.4 5.2 %all-to-all-start = ((s32[8,1,4]{2,1,0:T(1,128)}), s32[8,1,4]{2,1,0:T(1,128)S(1)}, u32[]{:S(2)}, u32[]{:S(2)}) async-start(s32[8,1,4]{2,1,0:T(1,128)} %broadcast_in_dim.96), calls=%async_computation.1 | async-start | bytes 8192 | tf_op jit(solution)/shard_map/all_to_all | solution.py:457
  13.6 0.0 reduce-scatter.2.cloned.1.call-start
  14.3 0.0 copy-start.1
  14.3 2.0 fusion.1
  16.4 2.1 fusion.3
  18.5 0.0 copy-done.1
  18.5 1.1 convolution_convert_fusion.2
  19.6 1.4 pad_maximum_fusion.x_ref
  21.0 187.8 %shard_map.131 = (bf16[512,1792]{1,0:T(8,128)(2,1)}, bf16[512,896]{1,0:T(8,128)(2,1)}) custom-call(bf16[128,7552]{1,0:T(8,128)(2,1)} %pad_maximum_fusion.x_ref, bf16[896,896]{1,0:T(8,128)(2,1)} %wk_ref.1, bf16[896,896]{1,0:T(8,128)(2,1)} %wv_ref.1, bf16[896,896]{1,0:T(8,128)(2,1)} %wq_ref.1, bf16[3,128,896]{2,1,0:T(8,128)(2,1)} %up_ref.1), custom_call_target="tpu_custom_call" | custom-call | flops 19730006016 | bytes 38535168 | tf_op jit(solution)/shard_map/pallas_call | solution.py:291
  208.8 0.0 copy-start
  208.8 2.3 copy.27
  211.2 0.0 copy-done
  211.2 1.1 fusion.17
  212.2 2.2 copy.28
  214.5 1.3 copy.26
  215.8 0.0 copy-done.4
  215.8 0.2 fusion.10
  216.0 0.0 copy-start.3
  216.0 5.2 %fusion.18 = (f32[4,512]{1,0:T(4,128)S(1)}, f32[4,512,512]{1,2,0:T(8,128)}) fusion(pred[512,512]{0,1:T(8,128)(4,1)S(1)} %fusion.10, bf16[512,4,224]{0,2,1:T(8,128)(2,1)} %bitcast.23, bf16[512,4,224]{0,2,1:T(8,128)(2,1)} %bitcast.25), kind=kOutput, calls=%fused_computation.46 | convolution fusion | flops 473956864 | bytes 6299648 | tf_op jit(solution)/shard_map/sub | solution.py:348
  221.2 0.0 copy-done.3
  221.2 2.8 select_convert_fusion
  224.1 8.3 %convolution_convert_fusion.1 = bf16[512,3584]{1,0:T(8,128)(2,1)} fusion(bf16[512,896]{0,1:T(8,128)(2,1)S(1)} %bitcast.27, bf16[896,3584]{1,0:T(8,128)(2,1)} %param.20), kind=kOutput, calls=%fused_computation.3 | convolution fusion | flops 3290169344 | bytes 11010048 | tf_op jit(solution)/shard_map/dot_general | solution.py:427
  232.3 0.0 reduce-scatter.2.cloned.1.call-update
  232.4 0.1 convert_reduce_fusion
  232.5 0.1 select_reduce_fusion
  232.6 0.1 iota_add_fusion
  232.6 0.1 compare_and_fusion
  232.7 0.1 add_minimum_fusion
  232.8 0.1 min.22
  232.9 0.3 broadcast_in_dim.101
  233.2 2.2 broadcast_in_dim.102
  235.4 0.3 broadcast_in_dim.97
  235.8 2.2 broadcast_in_dim.98
  237.9 3.1 %gather_fusion = bf16[512,1792]{1,0:T(8,128)(2,1)} fusion(bf16[512,1792]{1,0:T(8,128)(2,1)S(1)} %copy-done, s32[1024]{0:T(1024)S(1)} %pad_clamp_fusion), kind=kCustom, calls=%fused_computation | custom fusion | bytes 3672064 | tf_op jit(solution)/shard_map/jit(_take)/gather | solution.py:451
  241.1 3.5 %gather.7 = bf16[8,4,28672]{2,1,0:T(4,128)(2,1)S(1)} reshape(bf16[512,1792]{1,0:T(8,128)(2,1)} %gather_fusion) | data formatting | bytes 3670016 | tf_op jit(solution)/shard_map/jit(_take)/gather | solution.py:451
  244.6 0.0 copy-done.2
  244.6 4.7 %select_select_fusion = bf16[8,4,28672]{2,1,0:T(4,128)(2,1)} fusion(pred[8,4,28672]{2,1,0:T(4,128)(4,1)} %broadcast_in_dim.98, pred[8,4,28672]{2,1,0:T(4,128)(4,1)S(1)} %copy-done.2, bf16[8,4,28672]{2,1,0:T(4,128)(2,1)S(1)} %gather.7), kind=kLoop, calls=%fused_computation.19 | loop fusion | flops 1835008 | bytes 5505024 | tf_op jit(solution)/shard_map/jit(_where)/select_n | solution.py:452
  249.3 0.0 all-to-all-done
  249.3 3.6 %all-to-all-start.1 = ((bf16[8,4,28672]{2,1,0:T(4,128)(2,1)}), bf16[8,4,28672]{2,1,0:T(4,128)(2,1)S(1)}, u32[]{:S(2)}, u32[]{:S(2)}) async-start(bf16[8,4,28672]{2,1,0:T(4,128)(2,1)} %select_select_fusion), calls=%async_computation.2 | async-start | bytes 3670016 | tf_op jit(solution)/shard_map/all_to_all | solution.py:456
  252.9 0.5 broadcast.150
  253.4 0.6 reduce.3
  254.0 0.1 eq.48
  254.1 22.6 %all-to-all-done.1 = bf16[8,4,28672]{2,1,0:T(4,128)(2,1)S(1)} async-done(((bf16[8,4,28672]{2,1,0:T(4,128)(2,1)}), bf16[8,4,28672]{2,1,0:T(4,128)(2,1)S(1)}, u32[]{:S(2)}, u32[]{:S(2)}) %all-to-all-start.1) | async-done | bytes 1835040 | tf_op jit(solution)/shard_map/all_to_all | solution.py:456
  276.7 1.5 reshape.199
  278.1 2.3 convolution_convert_fusion
  280.4 2.4 reshape.200
  282.8 18.3 %reduce-scatter.2.cloned.1.call-done = bf16[128,3584]{1,0:T(8,128)(2,1)} async-done(((bf16[512,3584]{1,0:T(8,128)(2,1)}), bf16[128,3584]{1,0:T(8,128)(2,1)}) %reduce-scatter.2.cloned.1.call-update) | async-done | bytes 917520 | tf_op jit(solution)/shard_map/reduce_scatter | solution.py:426
  (7 shorter events, 0.0 us)
Async XLA Ops:
  8.4 240.9 %all-to-all-start = ((s32[8,1,4]{2,1,0:T(1,128)}), s32[8,1,4]{2,1,0:T(1,128)S(1)}, u32[]{:S(2)}, u32[]{:S(2)}) async-start(s32[8,1,4]{2,1,0:T(1,128)} %broadcast_in_dim.96), calls=%async_computation.1 | async-start | bytes 8192 | tf_op jit(solution)/shard_map/all_to_all | solution.py:457
  13.6 287.5 %reduce-scatter.2.cloned.1.call-start = ((), (), s32[]{:S(2)}) async-start(), calls=%async_computation.3 | async-start | bytes 4587520 | tf_op jit(solution)/shard_map/reduce_scatter | solution.py:426
  14.3 4.2 %copy-start.1 = (bf16[7168,384]{1,0:T(8,128)(2,1)S(1)}, bf16[7168,384]{1,0:T(8,128)(2,1)}, u32[]{:S(2)}) copy-start(bf16[7168,384]{1,0:T(8,128)(2,1)} %param.18) | copy-start | bytes 16515076
  208.8 2.4 copy-start
  212.2 3.5 %copy-start.4 = (s32[512]{0:T(512)S(1)}, s32[512]{0:T(512)}, u32[]{:S(2)}) copy-start(s32[512]{0:T(512)} %param.21) | copy-start | bytes 6148
  216.0 5.2 %copy-start.3 = (bf16[512,896]{0,1:T(8,128)(2,1)S(1)}, bf16[512,896]{0,1:T(8,128)(2,1)}, u32[]{:S(2)}) copy-start(bf16[512,896]{0,1:T(8,128)(2,1)} %copy.26) | copy-start | bytes 2752516
  241.1 3.6 %copy-start.2 = (pred[8,4,28672]{2,1,0:T(4,128)(4,1)S(1)}, pred[8,4,28672]{2,1,0:T(4,128)(4,1)}, u32[]{:S(2)}) copy-start(pred[8,4,28672]{2,1,0:T(4,128)(4,1)} %broadcast_in_dim.102) | copy-start | bytes 2752516
  249.3 27.4 %all-to-all-start.1 = ((bf16[8,4,28672]{2,1,0:T(4,128)(2,1)}), bf16[8,4,28672]{2,1,0:T(4,128)(2,1)S(1)}, u32[]{:S(2)}, u32[]{:S(2)}) async-start(bf16[8,4,28672]{2,1,0:T(4,128)(2,1)} %select_select_fusion), calls=%async_computation.2 | async-start | bytes 3670016 | tf_op jit(solution)/shard_map/all_to_all | solution.py:456
Sparse Core Ops, SparseCore 0:
  232.5 68.5 reduce-scatter.1

commit v2 on v1

--- a/solution.py
+++ b/solution.py
@@ -203,7 +203,6 @@
     take_diag(0)
     token_wait_recv(1)
     token_start(2)
-    token_wait_recv(2)
     x_local.wait()
     for m in range(3):
         local_copy(m).wait()
@@ -213,63 +212,74 @@
         for j in range(4):
             sib_copy(m, j).wait_recv()
 
-    rows = q_ref.shape[0]
+    pair = z // 2
+    rows = q_ref.shape[0] // 2
     rank = up_ref.shape[1]
-
-    def tokens(r):
+    adapter = (1, 2, 0)
+    wide = 256
+
+    def slots(side):
+        return pl.ds(2 * side, 2)
+
+    def tokens(side, r):
         at = pl.multiple_of(flip(d, r) * depth, 128)
-        return xs[:, :, pl.ds(at, depth)].reshape(rows, depth)
-
-    adapter = (1, 2, 0)
-
-    def low(m):
+        return xs[slots(side), :, pl.ds(at, depth)].reshape(rows, depth)
+
+    def low(side, m):
         at = din + adapter[m] * rank
-        return xs[:, :, at : at + rank].reshape(rows, rank)
-
-    for m in range(2):
-        for c in range(cols // 128):
-            lo = m * cols + c * 128
-            acc[:, pl.ds(lo, 128)] = jnp.dot(
-                low(m), up_ref[adapter[m], :, c * 128 : (c + 1) * 128], preferred_element_type=F32
+        return xs[slots(side), :, at : at + rank].reshape(rows, rank)
+
+    def start_acc(side, m, lo):
+        for c in range(0, cols, 128):
+            acc[:, lo + c : lo + c + 128] = jnp.dot(
+                low(side, m), up_ref[adapter[m], :, c : c + 128], preferred_element_type=F32
             )
 
-    wide = 256
-
-    def kv_tile(t, carry):
-        at = pl.multiple_of(t * wide, 128)
-        tile = pl.ds(at, wide)
-
-        def add(r, c):
-            acc[:, tile] += jnp.dot(tokens(r), ws[r, :, tile], preferred_element_type=F32)
+    def keys_values(side):
+        at_rows = pl.ds(pl.multiple_of(side * rows, rows), rows)
+        for m in range(2):
+            start_acc(side, m, m * cols)
+
+        def kv_tile(t, carry):
+            tile = pl.ds(pl.multiple_of(t * wide, 128), wide)
+
+            def add(r, c):
+                acc[:, tile] += jnp.dot(
+                    tokens(side, r), ws[r, :, tile], preferred_element_type=F32
+                )
+                return c
+
+            lax.fori_loop(0, 8, add, 0)
+            kv_ref[at_rows, tile] = acc[:, tile].astype(BF)
+            return carry
+
+        lax.fori_loop(0, 2 * cols // wide, kv_tile, 0)
+
+    def queries(side):
+        at_rows = pl.ds(pl.multiple_of(side * rows, rows), rows)
+        start_acc(side, 2, 0)
+
+        def q_add(r, c):
+            for lo in range(0, cols, wide):
+                width = min(wide, cols - lo)
+                acc[:, lo : lo + width] += jnp.dot(
+                    tokens(side, r),
+                    ws[r, :, 2 * cols + lo : 2 * cols + lo + width],
+                    preferred_element_type=F32,
+                )
             return c
 
-        lax.fori_loop(0, 8, add, 0)
-        kv_ref[:, tile] = acc[:, tile].astype(BF)
-        return carry
-
-    lax.fori_loop(0, 2 * cols // wide, kv_tile, 0)
-
-    for c in range(cols // 128):
-        acc[:, c * 128 : (c + 1) * 128] = jnp.dot(
-            low(2), up_ref[adapter[2], :, c * 128 : (c + 1) * 128], preferred_element_type=F32
-        )
-    for j in range(3):
+        lax.fori_loop(0, 8, q_add, 0)
+        q_ref[at_rows, :] = acc[:, :cols].astype(BF)
+
+    keys_values(pair)
+    take_diag(2)
+    for j in range(4):
         sib_copy(2, j).wait_recv()
-
-    def q_add(r, c):
-        for lo in range(0, cols, wide):
-            width = min(wide, cols - lo)
-            acc[:, lo : lo + width] += jnp.dot(
-                tokens(r), ws[r, :, 2 * cols + lo : 2 * cols + lo + width], preferred_element_type=F32
-            )
-        return c
-
-    lax.fori_loop(0, 6, q_add, 0)
-    take_diag(2)
-    q_add(6, 0)
-    sib_copy(2, 3).wait_recv()
-    q_add(7, 0)
-    q_ref[...] = acc[:, :cols].astype(BF)
+    queries(pair)
+    token_wait_recv(2)
+    keys_values(1 - pair)
+    queries(1 - pair)
 
     for step in range(n_z - 1):
         token_wait_send(step)
@@ -299,7 +309,7 @@
         scratch_shapes=[
             pltpu.VMEM((n_z,) + x.shape, BF),
             pltpu.VMEM((8, depth, 3 * cols), BF),
-            pltpu.VMEM((rows, 2 * cols), F32),
+            pltpu.VMEM((rows // 2, 2 * cols), F32),
             dma((4,)),
             dma((2, 3)),
             dma((2, 3)),
@@ -321,6 +331,66 @@
 
 epsilon = 1e-05
 negative = -1e30
+
+
+def attend_kernel(live_ref, q_ref, kv_ref, seg_col_ref, seg_row_ref, out_w_ref, out_ref, att):
+    rows, cols = q_ref.shape
+    count = 128
+    live = live_ref[0]
+    key_at = lax.broadcasted_iota(jnp.int32, (count, rows), 1)
+
+    @pl.loop(0, rows // count)
+    def _(i):
+        at = pl.ds(pl.multiple_of(i * count, count), count)
+        query_at = i * count + lax.broadcasted_iota(jnp.int32, (count, rows), 0)
+        allowed = (
+            (seg_col_ref[at, :] == seg_row_ref[...]) & (key_at <= query_at) & (key_at < live)
+        )
+        for h in range(cols // HD):
+            lo = h * HD // 128 * 128
+            hi = -(-(h + 1) * HD // 128) * 128
+            col = lo + lax.broadcasted_iota(jnp.int32, (count, hi - lo), 1)
+            mine = (col >= h * HD) & (col < (h + 1) * HD)
+            q = jnp.where(mine, q_ref[at, lo:hi], jnp.zeros((), BF))
+            scores = lax.dot_general(
+                q, kv_ref[:, lo:hi], (((1,), (1,)), ((), ())), preferred_element_type=F32
+            ) / math.sqrt(HD)
+            scores = jnp.where(allowed, scores, negative)
+            expo = jnp.exp(scores - jnp.max(scores, axis=-1, keepdims=True))
+            weights = (expo / jnp.sum(expo, axis=-1, keepdims=True)).astype(BF)
+            mixed = jnp.dot(weights, kv_ref[:, cols + lo : cols + hi], preferred_element_type=F32)
+            row = i * count + lax.broadcasted_iota(jnp.int32, (count, hi - lo), 0)
+            mixed = jnp.where(row < live, mixed, 0.0).astype(BF)
+            if h:
+                mixed = jnp.where(mine, mixed, att[at, lo:hi])
+            att[at, lo:hi] = mixed
+
+    wide = 256
+
+    @pl.loop(0, out_w_ref.shape[1] // wide)
+    def _(t):
+        tile = pl.ds(pl.multiple_of(t * wide, wide), wide)
+        out_ref[:, tile] = jnp.dot(
+            att[...], out_w_ref[:, tile], preferred_element_type=F32
+        ).astype(BF)
+
+
+def attend_project(query, stacked, segment, live, out_w):
+    rows, cols = query.shape
+    vmem = pl.BlockSpec(memory_space=pltpu.VMEM)
+    return pl.pallas_call(
+        attend_kernel,
+        out_shape=jax.ShapeDtypeStruct((rows, out_w.shape[1]), BF),
+        in_specs=[pl.BlockSpec(memory_space=pltpu.SMEM)] + [vmem] * 5,
+        out_specs=vmem,
+        scratch_shapes=[pltpu.VMEM((rows, cols), BF)],
+        compiler_params=pltpu.CompilerParams(vmem_limit_bytes=32 * 1024 * 1024),
+        cost_estimate=pl.CostEstimate(
+            flops=2 * rows * cols * (2 * rows + out_w.shape[1]),
+            bytes_accessed=2 * (3 * rows * cols + (cols + rows) * out_w.shape[1]),
+            transcendentals=rows * rows * (cols // HD),
+        ),
+    )(live, query, stacked, segment[:, None], segment[None, :], out_w)
 
 
 def normalize(hidden_state_input, token_embedding_input, input_norm_gain):
@@ -374,7 +444,9 @@
     ).astype(jnp.bfloat16)
     dp, n_z = lax.axis_size("dp"), lax.axis_size("tensor")
     depth = query_projection_weight.shape[0]
-    if dp == 8 and n_z == 4:
+    fast = dp == 8 and n_z == 4
+    all_rows = lax.all_gather(request_cache_row, "dp", axis=0, tiled=True)
+    if fast:
         own = jnp.concatenate([normalized_hidden, adapter_update], 1)
         stacked, query = project(
             own,
@@ -415,22 +487,23 @@
     stream = query.shape[0]
     position = jnp.arange(stream, dtype=jnp.int32)
     live = live_token_length[0]
-    block = min(512, stream)
-    attended_parts = []
-    for block_index in range(stream // block):
-        first = block_index * block
-        attended_parts.append(
-            attend_block(query, keys, values, segment, position, live, first, block, stream)
-        )
-    attended = jnp.concatenate(attended_parts, 0)
-    block_out = lax.psum_scatter(
-        jnp.dot(attended, output_projection_weight, preferred_element_type=jnp.float32).astype(
-            jnp.bfloat16
-        ),
-        "tensor",
-        scatter_dimension=0,
-        tiled=True,
-    )
+    if fast:
+        partial = attend_project(
+            query, stacked, segment, live_token_length, output_projection_weight
+        )
+    else:
+        block = min(512, stream)
+        attended_parts = []
+        for block_index in range(stream // block):
+            first = block_index * block
+            attended_parts.append(
+                attend_block(query, keys, values, segment, position, live, first, block, stream)
+            )
+        attended = jnp.concatenate(attended_parts, 0)
+        partial = jnp.dot(
+            attended, output_projection_weight, preferred_element_type=jnp.float32
+        ).astype(jnp.bfloat16)
+    block_out = lax.psum_scatter(partial, "tensor", scatter_dimension=0, tiled=True)
     requests = request_cache_row.shape[0]
     longest = stream // requests
     groups = lax.axis_size("dp")
@@ -451,14 +524,10 @@
     taken = jnp.take(stacked, source_rows.reshape(-1), axis=0)
     taken = jnp.where(alive_mask.reshape(-1)[:, None], taken, jnp.zeros((), jnp.bfloat16))
     taken = taken.reshape(groups, requests, piece_len * 2 * head_cols)
-    row_send = jnp.broadcast_to(request_cache_row[None, :], (groups, requests))
-    received, received_rows = (
-        lax.all_to_all(taken, "dp", split_axis=0, concat_axis=0, tiled=True),
-        lax.all_to_all(row_send, "dp", split_axis=0, concat_axis=0, tiled=True),
-    )
+    received = lax.all_to_all(taken, "dp", split_axis=0, concat_axis=0, tiled=True)
     total_reqs = groups * requests
     placing = (
-        received_rows.reshape(-1)[:, None] == jnp.arange(total_reqs, dtype=jnp.int32)[None, :]
+        all_rows[:, None] == jnp.arange(total_reqs, dtype=jnp.int32)[None, :]
     ).astype(jnp.bfloat16)
     flat_received = received.reshape(total_reqs, piece_len * 2 * head_cols)
     cache_rows = lax.dot_general(

time: 309 us -> 314 us (1.016)
  Pallas kernels: 188 us -> 216 us
  waiting for transfers between devices: 40.9 us -> 16 us
  blocking collectives: 0 us -> 24.5 us
  matrix products: 19.7 us -> 3.37 us
  starting transfers between devices: 8.81 us -> 3.77 us
    unnamed x0 -> x1, blocking collectives: none -> 24.5 us
    all_to_all x1, waiting for transfers between devices: 22.6 us -> 0.01 us  [body(): lax.all_to_all(taken, 'dp', split_axis=0, concat_axis=0, tiled=True)]
    pallas_call x1, Pallas kernels: 188 us -> 202 us  [project(): pl.pallas_call(functools.partial(project_kernel, depth, n_z, din), out_sh...]
    pallas_call x0 -> x1, Pallas kernels: none -> 13.9 us  [attend_project(): pl.pallas_call(attend_kernel, out_shape=jax.ShapeDtypeStruct((rows, out_w...]
    dot_general x2 -> x0, matrix products: 11.1 us -> none  [the longest x1 8.28 us: body(): jnp.dot(attended, output_projection_weight, preferred_element_type=jnp.fl...]
    unnamed x10 -> x25, local copies, waits for them, and re-layouts: 0.02 us -> 8.19 us
    sub x1 -> x0, matrix products: 5.19 us -> none  [attend_block(): expo = jnp.exp(scores - top)]
    all_to_all x1 -> x0, starting transfers between devices: 5.17 us -> none  [body(): lax.all_to_all(row_send, 'dp', split_axis=0, concat_axis=0, tiled=True)]
  transfers between devices with their start and end apart: 3 -> 2, of which waited for: 2 -> 1; matrix products, arithmetic and copies ran while one was open for 18% -> 8% of each run, Pallas kernels for 61% -> 0%
where the time goes in v2:
time: 314 us; the launch traced here: 313 us
  Pallas kernels  216 us (69%)
  blocking collectives  24.5 us (8%)
  local copies, waits for them, and re-layouts  23.9 us (8%)
  waiting for transfers between devices  16 us (5%)
  between operations  15.5 us (5%)
  other arithmetic  10.6 us (3%)
  starting transfers between devices  3.77 us (1%)
  matrix products  3.37 us (1%)
    pallas_call x1, Pallas kernels, project(): pl.pallas_call(functools.partial(project_kernel, depth, n_z, din), out_sh...  202 us
    unnamed x1, blocking collectives  24.5 us
    reduce_scatter x1, waiting for transfers between devices, body(): lax.psum_scatter(partial, 'tensor', scatter_dimension=0, tiled=True)  16 us
    pallas_call x1, Pallas kernels, attend_project(): pl.pallas_call(attend_kernel, out_shape=jax.ShapeDtypeStruct((rows, out_w...  13.9 us
    unnamed x25, local copies, waits for them, and re-layouts  8.19 us
    gather x2, local copies, waits for them, and re-layouts, body(): taken = jnp.take(stacked, source_rows.reshape(-1), axis=0)  6.68 us
  transfers between devices with their start and end apart: 2, of which 1 were waited for; matrix products, arithmetic and copies ran while one was open for 8% of the time, Pallas kernels for 0%

profile of v2, /device:TPU:0, one launch (start us, length us, event | category | flops | bytes accessed | tf_op | source)
XLA Modules:
  0.0 313.3 jit_solution(3534085444923234583)
XLA Ops:
  7.2 0.0 copy-start.8
  7.2 0.0 reduce-scatter.2.cloned.1.call-start
  7.9 0.0 copy-start.6
  7.9 2.0 fusion
  9.9 0.0 copy-done.8
  9.9 2.1 fusion.2
  12.0 0.0 copy-done.6
  12.0 1.1 convolution_convert_fusion.1
  13.2 0.0 copy-start.3
  13.2 1.4 pad_maximum_fusion.x_ref
  14.6 0.0 copy-done.3
  14.6 0.1 copy.15.seg_col_ref
  14.7 201.8 %shard_map.131 = (bf16[512,1792]{1,0:T(8,128)(2,1)}, bf16[512,896]{1,0:T(8,128)(2,1)}) custom-call(bf16[128,7552]{1,0:T(8,128)(2,1)} %pad_maximum_fusion.x_ref, bf16[896,896]{1,0:T(8,128)(2,1)} %wk_ref.1, bf16[896,896]{1,0:T(8,128)(2,1)} %wv_ref.1, bf16[896,896]{1,0:T(8,128)(2,1)} %wq_ref.1, bf16[3,128,896]{2,1,0:T(8,128)(2,1)} %up_ref.1), custom_call_target="tpu_custom_call" | custom-call | flops 19730006016 | bytes 38535168 | tf_op jit(solution)/shard_map/pallas_call | solution.py:301
  216.5 0.0 copy-start
  216.5 1.5 copy-done
  218.0 0.0 copy-start.4
  218.0 2.8 copy-done.4
  220.8 1.2 copy-done.5
  222.0 13.9 %shard_map.132 = bf16[512,3584]{1,0:T(8,128)(2,1)S(1)} custom-call(s32[1]{0:T(128)} %copy.17.live_ref, bf16[512,896]{1,0:T(8,128)(2,1)S(1)} %copy-done.5, bf16[512,1792]{1,0:T(8,128)(2,1)S(1)} %copy-done, s32[512,1]{1,0:T(8,128)S(1)} %copy.15.seg_col_ref, s32[1,512]{1,0:T(1,128)S(1)} %bitcast.14, bf16[896,3584]{1,0:T(8,128)(2,1)S(1)} %copy-done.4), custom_call_target="tpu_custom_call" | custom-call | flops 4227858432 | bytes 12845056 | tf_op jit(solution)/shard_map/pallas_call | solution.py:381
  235.9 0.0 copy-start.2
  235.9 1.8 copy-done.2
  237.7 0.0 reduce-scatter.2.cloned.1.call-update
  237.8 0.1 iota_add_fusion
  237.8 0.1 convert_reduce_fusion
  238.0 0.1 select_reduce_fusion
  238.0 0.1 compare_and_fusion
  238.1 0.1 add_minimum_fusion
  238.2 0.3 broadcast_in_dim.62
  238.5 2.2 broadcast_in_dim.63
  240.7 0.3 broadcast_in_dim.66
  241.0 2.2 broadcast_in_dim.67
  243.2 0.1 min.22
  243.3 0.0 copy-done.1
  243.4 3.1 %gather_fusion = bf16[512,1792]{1,0:T(8,128)(2,1)} fusion(bf16[512,1792]{1,0:T(8,128)(2,1)S(1)} %copy-done.1, s32[1024]{0:T(1024)S(1)} %pad_clamp_fusion), kind=kCustom, calls=%fused_computation | custom fusion | bytes 3672064 | tf_op jit(solution)/shard_map/jit(_take)/gather | solution.py:524
  246.5 3.5 %gather.7 = bf16[8,4,28672]{2,1,0:T(4,128)(2,1)S(1)} reshape(bf16[512,1792]{1,0:T(8,128)(2,1)} %gather_fusion) | data formatting | bytes 3670016 | tf_op jit(solution)/shard_map/jit(_take)/gather | solution.py:524
  250.0 0.0 copy-done.7
  250.1 4.7 %select_select_fusion = bf16[8,4,28672]{2,1,0:T(4,128)(2,1)} fusion(pred[8,4,28672]{2,1,0:T(4,128)(4,1)S(1)} %copy-done.7, pred[8,4,28672]{2,1,0:T(4,128)(4,1)} %broadcast_in_dim.67, bf16[8,4,28672]{2,1,0:T(4,128)(2,1)S(1)} %gather.7), kind=kLoop, calls=%fused_computation.9 | loop fusion | flops 1835008 | bytes 5505024 | tf_op jit(solution)/shard_map/jit(_where)/select_n | solution.py:525
  254.7 3.7 %all-to-all-start = ((bf16[8,4,28672]{2,1,0:T(4,128)(2,1)}), bf16[8,4,28672]{2,1,0:T(4,128)(2,1)S(1)}, u32[]{:S(2)}, u32[]{:S(2)}) async-start(bf16[8,4,28672]{2,1,0:T(4,128)(2,1)} %select_select_fusion), calls=%async_computation.1 | async-start | bytes 3670016 | tf_op jit(solution)/shard_map/all_to_all | solution.py:527
  258.5 0.0 copy-done.10
  258.5 0.6 dynamic-slice
  259.8 0.0 copy-done.9
  259.8 0.2 dynamic-update-slice
  260.0 24.5 %all-reduce = s32[32]{0:T(128)S(1)} all-reduce(s32[32]{0:T(128)S(1)} %dynamic-update-slice), channel_id=1, replica_groups=mesh['dp'=8,'tensor'=4] {'dp'}, use_global_device_ids=true, to_apply=%add | all-reduce | flops 32 | bytes 256
  284.5 0.0 all-to-all-done
  284.5 1.5 reshape.111
  285.9 2.2 convolution_convert_fusion
  288.2 2.4 reshape.112
  290.5 16.0 %reduce-scatter.2.cloned.1.call-done = bf16[128,3584]{1,0:T(8,128)(2,1)} async-done(((bf16[512,3584]{1,0:T(8,128)(2,1)}), bf16[128,3584]{1,0:T(8,128)(2,1)}) %reduce-scatter.2.cloned.1.call-update) | async-done | bytes 917520 | tf_op jit(solution)/shard_map/reduce_scatter | solution.py:506
  (11 shorter events, 0.0 us)
Async XLA Ops:
  7.2 2.8 copy-start.8
  7.2 299.3 %reduce-scatter.2.cloned.1.call-start = ((), (), s32[]{:S(2)}) async-start(), calls=%async_computation.2 | async-start | bytes 4587520 | tf_op jit(solution)/shard_map/reduce_scatter | solution.py:506
  7.9 4.1 %copy-start.6 = (bf16[7168,384]{1,0:T(8,128)(2,1)S(1)}, bf16[7168,384]{1,0:T(8,128)(2,1)}, u32[]{:S(2)}) copy-start(bf16[7168,384]{1,0:T(8,128)(2,1)} %param.18) | copy-start | bytes 16515076
  13.2 1.4 copy-start.3
  216.5 1.5 copy-start
  218.0 2.8 copy-start.4
  220.8 1.2 copy-start.5
  235.9 1.8 copy-start.2
  240.7 2.6 copy-start.1
  246.5 3.6 %copy-start.7 = (pred[8,4,28672]{2,1,0:T(4,128)(4,1)S(1)}, pred[8,4,28672]{2,1,0:T(4,128)(4,1)}, u32[]{:S(2)}) copy-start(pred[8,4,28672]{2,1,0:T(4,128)(4,1)} %broadcast_in_dim.63) | copy-start | bytes 2752516
  254.7 3.8 %copy-start.10 = (u32[32]{0:T(128)S(1)}, u32[32]{0:T(128)}, u32[]{:S(2)}) copy-start(u32[32]{0:T(128)} %constant.33) | copy-start | bytes 388
  254.7 5.0 %copy-start.9 = (s32[4]{0:T(128)S(1)}, s32[4]{0:T(128)}, u32[]{:S(2)}) copy-start(s32[4]{0:T(128)} %param.23) | copy-start | bytes 52
  254.7 29.8 %all-to-all-start = ((bf16[8,4,28672]{2,1,0:T(4,128)(2,1)}), bf16[8,4,28672]{2,1,0:T(4,128)(2,1)S(1)}, u32[]{:S(2)}, u32[]{:S(2)}) async-start(bf16[8,4,28672]{2,1,0:T(4,128)(2,1)} %select_select_fusion), calls=%async_computation.1 | async-start | bytes 3670016 | tf_op jit(solution)/shard_map/all_to_all | solution.py:527
Sparse Core Ops, SparseCore 0:
  237.9 68.5 reduce-scatter.1
